TPU v7x, 256 devices: a whole 4x4x8 slice. The times are simulated.
256 devices in a mesh: src: 64 (over y, x, z_hi, core), tgt: 4 (over z_lo).
Axes of the slice: x: 4, y: 4, z: 8 (z_hi: 2, z_lo: 4; z = z_hi * 4 + z_lo), core: 2. Of those that a mesh axis runs over, the one named last changes fastest.
Arguments:
- sources: bfloat16 [65536, 1024], P('src'), may hold values from -16 to 16
- targets: bfloat16 [8192, 1024], P(('src', 'tgt')), may hold values from -40 to 40
Outputs:
- row_best: float32 [65536], P('src')
- col_best: float32 [8192], P(('src', 'tgt'))
All inputs are finite; a program needn't handle non-finite values.
Results may differ from a plain program's by a relative error of at most 0.00096.
Values may be sent and summed in bfloat16 or wider, within the bound.
A program may use at most 64 MiB of HBM per device.

v0:
```python
import math

import jax
import jax.numpy as jnp
from jax import lax
from jax.sharding import PartitionSpec as P

sharpness_factor = 0.05


def unit_rows(matrix):
    values = matrix.astype(jnp.float32)
    scale = lax.rsqrt(jnp.mean(values * values, axis=1, keepdims=True) + 1e-06)
    return (values * scale / math.sqrt(matrix.shape[1])).astype(jnp.bfloat16)


def angle_agreement_table(target_positions, query_direction_list):
    return lax.dot_general(
        target_positions,
        query_direction_list,
        (((1,), (1,)), ((), ())),
        preferred_element_type=jnp.float32,
    )


def blocked(update, totals, panel_piece):
    length = panel_piece.shape[0]
    stride = math.gcd(length, 256)

    def advance(index_block, running):
        target_positions = lax.dynamic_slice_in_dim(panel_piece, index_block * stride, stride, 0)
        return update(running, target_positions, index_block * stride)

    return lax.fori_loop(0, length // stride, advance, totals)


def local(sources, targets):
    query_direction_list = unit_rows(sources)
    target_unit = unit_rows(targets)
    src_count = lax.axis_size("src")
    tgt_count = lax.axis_size("tgt")
    rows_here = query_direction_list.shape[0]
    piece_rows = target_unit.shape[0]
    group_rows = piece_rows * src_count

    def first_update(totals, target_positions, offset):
        row_totals, col_totals = totals
        nearby_shares = jnp.exp(
            angle_agreement_table(target_positions, query_direction_list) / sharpness_factor
        )
        col_totals = lax.dynamic_update_slice_in_dim(
            col_totals, jnp.sum(nearby_shares, axis=1), offset, 0
        )
        return (row_totals + jnp.sum(nearby_shares, axis=0), col_totals)

    start_sums = (jnp.zeros((rows_here,), jnp.float32), jnp.zeros((group_rows,), jnp.float32))
    row_totals, col_totals = blocked(
        first_update, start_sums, lax.all_gather(target_unit, "src", axis=0, tiled=True)
    )
    src_index = lax.axis_index("src")
    row_totals = lax.psum(row_totals, "tgt")
    col_totals = lax.psum(col_totals, "src")
    left_side_divisor = jnp.log(row_totals / (group_rows * tgt_count))
    target_side_divisor = jnp.log(col_totals / (rows_here * src_count))

    def second_update(totals, target_positions, offset):
        row_top, col_top = totals
        divisor_segment = lax.dynamic_slice_in_dim(
            target_side_divisor, offset, target_positions.shape[0], 0
        )
        ratio_criterion = angle_agreement_table(
            target_positions, query_direction_list
        ) - 0.5 * sharpness_factor * (divisor_segment[:, None] + left_side_divisor[None, :])
        col_top = lax.dynamic_update_slice_in_dim(
            col_top, jnp.max(ratio_criterion, axis=1), offset, 0
        )
        return (jnp.maximum(row_top, jnp.max(ratio_criterion, axis=0)), col_top)

    start_tops = (
        jnp.full((rows_here,), -1e30, jnp.float32),
        jnp.full((group_rows,), -1e30, jnp.float32),
    )
    row_top, col_top = blocked(
        second_update, start_tops, lax.all_gather(target_unit, "src", axis=0, tiled=True)
    )
    row_best = lax.pmax(row_top, "tgt")
    reduced = lax.pmax(col_top, "src")
    col_best = lax.dynamic_slice_in_dim(reduced, src_index * piece_rows, piece_rows, 0)
    return (row_best, col_best)


def solution(mesh):
    in_specs = (P("src", None), P(("src", "tgt"), None))
    out_specs = (P("src"), P(("src", "tgt")))
    return jax.shard_map(local, mesh=mesh, in_specs=in_specs, out_specs=out_specs, check_vma=False)
```

profile of v0, /device:TPU:1, one launch (start us, length us, event | category | flops | bytes accessed | tf_op | source)
XLA Modules:
  0.0 579.9 jit_solution(12723610429312779237)
XLA Ops:
  7.2 1.0 fusion.8
  8.2 1.6 fusion.10
  9.8 2.1 fusion.5
  11.9 2.1 fusion.7
  14.0 94.7 %all-gather.2.cloned.1.call-done = bf16[2048,1024]{1,0:T(8,128)(2,1)} async-done(((bf16[32,1024]{1,0:T(8,128)(2,1)}), bf16[2048,1024]{1,0:T(8,128)(2,1)}) %all-gather.2.cloned.1.call-update) | async-done | bytes 4194320 | tf_op jit(solution)/shard_map/all_gather | solution.py:84
  108.7 17.8 %while.32 = (s32[]{:T(128)}, f32[1024]{0:T(1024)S(1)}, f32[2048]{0:T(1024)S(1)}, bf16[2048,1024]{1,0:T(8,128)(2,1)}, bf16[1024,1024]{1,0:T(8,128)(2,1)S(1)}, /*index=5*/s32[]{:T(128)}, s32[]{:T(128)}, s32[]{:T(128)}, s32[]{:T(128)}) while((s32[]{:T(128)}, f32[1024]{0:T(1024)S(1)}, f32[2048]{0:T(1024)S(1)}, ...), condition=%wide.region_5.0_spmd.clone, body=%wide.region_2.0_spmd.clone.sunk | while | flops 537658112 | bytes 2641061 | solution.py:34
  108.7 1.9 fusion.20
  110.9 1.9 fusion.20
  112.9 0.3 dynamic_update_slice.18
  113.2 1.9 fusion.20
  115.1 0.3 dynamic_update_slice.18
  115.4 1.9 fusion.20
  117.7 1.9 fusion.20
  119.9 1.9 fusion.20
  122.1 1.9 fusion.20
  124.3 1.9 fusion.20
  126.5 202.7 %psum.14 = f32[2048]{0:T(1024)S(1)} all-reduce(f32[2048]{0:T(1024)S(1)} %get-tuple-element.222), channel_id=1, replica_groups=mesh['src'=64,'tgt'=4] {'src'}, use_global_device_ids=true, to_apply=%region_6.0 | all-reduce | flops 2048 | bytes 16384 | tf_op jit(solution)/shard_map/psum | solution.py:62
  329.2 6.9 %psum.15 = f32[1024]{0:T(1024)S(1)} all-reduce(f32[1024]{0:T(1024)S(1)} %get-tuple-element.223), channel_id=1, replica_groups=mesh['src'=64,'tgt'=4] {'tgt'}, use_global_device_ids=true, to_apply=%region_7.0 | all-reduce | flops 1024 | bytes 8192 | tf_op jit(solution)/shard_map/psum | solution.py:61
  336.2 18.5 %while.33 = (s32[]{:T(128)}, f32[1024]{0:T(1024)S(1)}, f32[2048]{0:T(1024)S(1)}, bf16[2048,1024]{1,0:T(8,128)(2,1)}, bf16[1024,1024]{1,0:T(8,128)(2,1)S(1)}, /*i...) while((s32[]{:T(128)}, f32[1024]{0:T(1024)S(1)}, ...), condition=%wide.region_11.0_spmd.clone, body=%wide.region_8.0_spmd.clone.sunk | while | flops 538182400 | bytes 2648249 | solution.py:34
  336.3 2.0 fusion.22
  338.6 2.0 fusion.22
  340.6 0.3 dynamic_update_slice.19
  340.9 2.0 fusion.22
  343.3 2.0 fusion.22
  345.2 0.3 dynamic_update_slice.19
  345.6 2.0 fusion.22
  347.9 2.0 fusion.22
  350.2 2.0 fusion.22
  352.5 2.0 fusion.22
  354.7 8.4 %pmax.14 = f32[1024]{0:T(1024)} all-reduce(f32[1024]{0:T(1024)S(1)} %get-tuple-element.224), channel_id=1, replica_groups=mesh['src'=64,'tgt'=4] {'tgt'}, use_global_device_ids=true, to_apply=%region_12.0 | all-reduce | flops 1024 | bytes 8192 | tf_op jit(solution)/shard_map/pmax | solution.py:86
  363.1 209.4 %pmax.15 = f32[2048]{0:T(1024)S(1)} all-reduce(f32[2048]{0:T(1024)S(1)} %get-tuple-element.225), channel_id=1, replica_groups=mesh['src'=64,'tgt'=4] {'src'}, use_global_device_ids=true, to_apply=%region_13.0 | all-reduce | flops 2048 | bytes 16384 | tf_op jit(solution)/shard_map/pmax | solution.py:87
  572.5 0.6 dynamic_slice.24
  (46 shorter events, 3.9 us)
Async XLA Ops:
  7.2 101.5 %all-gather.2.cloned.1.call-start = ((), (), s32[]{:S(2)}) async-start(), calls=%async_computation | async-start | bytes 4259840 | tf_op jit(solution)/shard_map/all_gather | solution.py:84
Sparse Core Ops, SparseCore 0:
  11.5 97.1 all-gather.1
where the time goes:
time: 581 us; the launch traced here: 580 us
  blocking collectives  427 us (73%)
  waiting for transfers between devices  94.7 us (16%)
  matrix products  31.3 us (5%)
  between operations  14.1 us (2%)
  other arithmetic  6.86 us (1%)
    pmax x1, blocking collectives, local(): reduced = lax.pmax(col_top, 'src')  209 us
    psum x1, blocking collectives, local(): col_totals = lax.psum(col_totals, 'src')  203 us
    all_gather x1, waiting for transfers between devices, local(): lax.all_gather(target_unit, 'src', axis=0, tiled=True)  94.7 us
    dot_general x16, matrix products, angle_agreement_table(): lax.dot_general(target_positions, query_direction_list, (((1,), (1,)), ((...  31.3 us
  transfers between devices with their start and end apart: 1, of which 1 were waited for; matrix products, arithmetic and copies ran while one was open for 1% of the time, Pallas kernels for 0%

commit v1 on v0

v1 whole, which is shorter than its diff:
```python
import functools
import math

import jax
import jax.numpy as jnp
from jax import lax
from jax.experimental import pallas as pl
from jax.experimental.pallas import tpu as pltpu
from jax.sharding import PartitionSpec as P

MESH = pl.DeviceIdType.MESH
EXP_SCALE = 20.0 * math.log2(math.e)
HALF = 0.025
RING = 4
ROWS, DEPTH, PIECE = 1024, 1024, 32
LANES = 128
ORDER = ((0, 0), (0, -1), (0, 1), (1, 0), (0, 2), (1, -1), (1, 1), (1, 2))
VIA_PLUS = ((0, 1), (-1, 2))


def unit_rows(values):
    values = values.astype(jnp.float32)
    scale = lax.rsqrt(jnp.mean(values * values, axis=1, keepdims=True) + 1e-06)
    return (values * scale * (1.0 / 32.0)).astype(jnp.bfloat16)


def kernel(
    src_ref,
    tgt_ref,
    row_ref,
    col_ref,
    unit,
    piece,
    gathered,
    cosine,
    row_acc,
    row_bias,
    col_part,
    col_one,
    col_two,
    max_one,
    max_two,
    row_one,
    row_max,
    col_norm,
    row_norm,
    load_sem,
    recv_sem,
    pair_sem,
    send_sem,
    small_send,
    small_recv,
):
    s = lax.axis_index("src")
    t = lax.axis_index("tgt")
    c = s % 2
    zh = (s // 2) % 2
    x = (s // 4) % 4
    y = s // 16
    a = x + c * (y - x)
    b = y + c * (x - y)

    def device(y, x, zh, c, t):
        return (((y * 4 + x) * 2 + zh) * 2 + c, t)

    def moved(da, db):
        aa, bb = (a + da + RING) % RING, (b + db + RING) % RING
        return device(bb + c * (aa - bb), aa + c * (bb - aa), zh, c, t)

    other_core = device(y, x, zh, 1 - c, t)
    other_plane = device(y, x, 1 - zh, c, 3 - t)

    load = pltpu.make_async_copy(src_ref, unit, load_sem.at[0])
    load.start()
    load_piece = pltpu.make_async_copy(tgt_ref, piece, load_sem.at[1])
    load_piece.start()

    me_one, me_two = x * 2 + c, y * 2 + zh
    peers_one, peers_two, peers_row = [], [], []
    for i in range(1, 8):
        p = (me_one + i) % 8
        peers_one.append(device(y, p // 2, zh, p % 2, t))
        p = (me_two + i) % 8
        q = p % 2
        other = (q - zh) * (q - zh)
        peers_two.append(device(p // 2, x, q, c, t + other * (3 - 2 * t)))
    for i in range(1, 4):
        peers_row.append(device(y, x, zh, c, (t + i) % 4))

    barrier = pltpu.get_barrier_semaphore()
    for peer in peers_one + peers_two + peers_row:
        pl.semaphore_signal(barrier, inc=1, device_id=peer, device_id_type=MESH)

    def plane_of(p):
        return zh if p == 0 else 1 - zh

    def ring(v, d):
        return (v + d + RING) % RING

    load_piece.wait()
    gathered[c, zh, b, a] = unit_rows(piece[...])
    pl.semaphore_wait(barrier, 17)

    sends = []

    def chunk_copy(p, db, da, to, send):
        pp, bb, aa = plane_of(p), ring(b, db), ring(a, da)
        slot = gathered.at[c, pp, bb, aa]
        return pltpu.make_async_remote_copy(
            src_ref=slot,
            dst_ref=slot,
            send_sem=send_sem.at[send],
            recv_sem=recv_sem.at[(pp * RING + bb) * RING + aa],
            device_id=to,
            device_id_type=MESH,
        )

    def forward(p, db, da, to):
        copy = chunk_copy(p, db, da, to, len(sends))
        copy.start()
        sends.append(copy)

    def arrived(p, db, da):
        chunk_copy(p, db, da, other_core, 0).wait_recv()

    def pair_copy(step, mine):
        p, db = ORDER[step]
        core = c if mine else 1 - c
        slot = gathered.at[core, plane_of(p), ring(b if mine else a, db)]
        return pltpu.make_async_remote_copy(
            src_ref=slot,
            dst_ref=slot,
            send_sem=send_sem.at[31 + step],
            recv_sem=pair_sem.at[step],
            device_id=other_core,
            device_id_type=MESH,
        )

    plus_a, minus_a, plus_b, minus_b = moved(1, 0), moved(-1, 0), moved(0, 1), moved(0, -1)

    def spread(step):
        p, db = ORDER[step]
        for da in (0, -1, 1, 2):
            if (p, db, da) != (0, 0, 0):
                arrived(p, db, da)
            if db == 0:
                if da == 0:
                    forward(p, 0, 0, plus_a)
                    forward(p, 0, 0, minus_a)
                    if p == 0:
                        forward(p, 0, 0, other_plane)
                if da == -1 and p == 0:
                    forward(p, 0, da, plus_a)
                if da == 1 and p == 1:
                    forward(p, 0, da, minus_a)
                forward(p, 0, da, plus_b)
                forward(p, 0, da, minus_b)
            elif db == -1 and da in VIA_PLUS[p]:
                forward(p, db, da, plus_b)
            elif db == 1 and da not in VIA_PLUS[p]:
                forward(p, db, da, minus_b)
            if (p, db, da) == (0, 0, 0):
                prepare()
        copy = pair_copy(step, True)
        copy.start()
        return copy

    def prepare():
        load.wait()

        def body(i, carry):
            rows = pl.ds(pl.multiple_of(i * 64, 64), 64)
            unit[rows, :] = unit_rows(unit[rows, :])
            return carry

        lax.fori_loop(0, ROWS // 64, body, 0)
        row_acc[...] = jnp.zeros_like(row_acc)

    def lines(step):
        p, db = ORDER[step]
        pp = plane_of(p)
        return (c * 2 + pp) * 4 + ring(b, db), ((1 - c) * 2 + pp) * 4 + ring(a, db)

    def multiply(step):
        p, db = ORDER[step]
        pair_copy(step, False).wait_recv()
        pp = plane_of(p)
        group = jnp.concatenate(
            [
                gathered[c, pp, ring(b, db)].reshape(LANES, DEPTH),
                gathered[1 - c, pp, ring(a, db)].reshape(LANES, DEPTH),
            ],
            axis=0,
        )
        mine, theirs = lines(step)
        block = 512

        def body(i, total):
            rows = pl.ds(pl.multiple_of(i * block, block), block)
            angle = lax.dot_general(
                unit[rows, :], group, (((1,), (1,)), ((), ())), preferred_element_type=jnp.float32
            )
            cosine[step, rows, :] = angle
            share = jnp.exp2(angle * EXP_SCALE)
            row_acc[rows, :] += share[:, :LANES] + share[:, LANES:]
            return total + jnp.sum(share.reshape(block // 8, 8, 2 * LANES), axis=0)

        total = lax.fori_loop(0, ROWS // block, body, jnp.zeros((8, 2 * LANES), jnp.float32))
        col_part[mine] = total[:, :LANES]
        col_part[theirs] = total[:, LANES:]

    pair_sends = [spread(0), spread(1)]
    for step in range(8):
        if step + 2 < 8:
            pair_sends.append(spread(step + 2))
        multiply(step)

    small = []

    def exchange(buffer, me, peers, base, width):
        for i, peer in enumerate(peers):
            copy = pltpu.make_async_remote_copy(
                src_ref=buffer.at[me],
                dst_ref=buffer.at[me],
                send_sem=small_send.at[base + i],
                recv_sem=small_recv.at[base + i],
                device_id=peer,
                device_id_type=MESH,
            )
            copy.start()
            small.append(copy)

    def collect(buffer, me, count, base, width):
        for i in range(count):
            slot = buffer.at[(me + width - 1 - i) % width]
            pltpu.make_async_remote_copy(
                src_ref=slot,
                dst_ref=slot,
                send_sem=small_send.at[base + i],
                recv_sem=small_recv.at[base + i],
                device_id=other_core,
                device_id_type=MESH,
            ).wait_recv()

    def columns(reduce, source):
        return reduce(source[...], axis=1)

    def rows_of(source, reduce):
        parts = []
        for i in range(8):
            block = source[i * LANES : (i + 1) * LANES, :]
            parts.append(reduce(block.T, axis=0, keepdims=True))
        return jnp.concatenate(parts, axis=0)

    col_one[me_one] = columns(jnp.sum, col_part)
    exchange(col_one, me_one, peers_one, 0, 8)
    row_one[t] = rows_of(row_acc, jnp.sum)
    exchange(row_one, t, peers_row, 14, 4)
    collect(col_one, me_one, 7, 0, 8)
    col_two[me_two] = jnp.sum(col_one[...], axis=0)
    exchange(col_two, me_two, peers_two, 7, 8)

    collect(row_one, t, 3, 14, 4)
    row_norm[...] = HALF * jnp.log(jnp.sum(row_one[...], axis=0) * (1.0 / 8192.0))
    for i in range(8):
        line = jnp.broadcast_to(row_norm[i : i + 1, :], (LANES, LANES))
        row_bias[i * LANES : (i + 1) * LANES, :] = line.T

    def col_body(i, tops):
        rows = pl.ds(pl.multiple_of(i * 32, 32), 32)
        bias = row_bias[rows, :]
        bias = jnp.concatenate([bias, bias], axis=1)
        new = []
        for step in range(8):
            value = (cosine[step, rows, :] - bias).reshape(4, 8, 2 * LANES)
            new.append(jnp.maximum(tops[step], jnp.max(value, axis=0)))
        return tuple(new)

    start = jnp.full((8, 2 * LANES), -1e30, jnp.float32)
    tops = lax.fori_loop(0, ROWS // 32, col_body, (start,) * 8)
    for step in range(8):
        mine, theirs = lines(step)
        col_part[mine] = tops[step][:, :LANES]
        col_part[theirs] = tops[step][:, LANES:]
    max_one[me_one] = columns(jnp.max, col_part)
    exchange(max_one, me_one, peers_one, 17, 8)

    collect(col_two, me_two, 7, 7, 8)
    col_norm[...] = HALF * jnp.log(jnp.sum(col_two[...], axis=0) * (1.0 / 65536.0))

    def row_body(i, carry):
        rows = pl.ds(pl.multiple_of(i * 32, 32), 32)
        top = None
        for step in range(8):
            mine, theirs = lines(step)
            value = cosine[step, rows, :]
            for part, line in ((value[:, :LANES], mine), (value[:, LANES:], theirs)):
                part = part - col_norm[pl.ds(line, 1), :]
                top = part if top is None else jnp.maximum(top, part)
        row_acc[rows, :] = top
        return carry

    lax.fori_loop(0, ROWS // 32, row_body, 0)
    row_max[t] = rows_of(row_acc, jnp.max)
    exchange(row_max, t, peers_row, 31, 4)

    collect(max_one, me_one, 7, 17, 8)
    max_two[me_two] = jnp.max(max_one[...], axis=0)
    exchange(max_two, me_two, peers_two, 24, 8)
    collect(row_max, t, 3, 31, 4)
    row_ref[...] = jnp.max(row_max[...], axis=0) - row_norm[...]
    collect(max_two, me_two, 7, 24, 8)
    best = jnp.max(max_two[...], axis=0) - col_norm[...]
    line = (c * 2 + zh) * 4 + b
    chosen = lax.broadcasted_iota(jnp.int32, (16, LANES), 0) == line
    best = jnp.sum(jnp.where(chosen, best, 0.0), axis=0, keepdims=True)
    out = jnp.zeros((1, PIECE), jnp.float32)
    for i in range(RING):
        out = jnp.where(a == i, best[:, i * PIECE : (i + 1) * PIECE], out)
    col_ref[...] = out

    for copy in sends + pair_sends + small:
        copy.wait_send()


def local(sources, targets):
    f32, bf16 = jnp.float32, jnp.bfloat16
    dma = pltpu.SemaphoreType.DMA
    row_best, col_best = pl.pallas_call(
        kernel,
        out_shape=(
            jax.ShapeDtypeStruct((8, LANES), f32),
            jax.ShapeDtypeStruct((1, PIECE), f32),
        ),
        in_specs=[pl.BlockSpec(memory_space=pl.ANY)] * 2,
        out_specs=(pl.BlockSpec(memory_space=pltpu.VMEM),) * 2,
        scratch_shapes=[
            pltpu.VMEM((ROWS, DEPTH), bf16),
            pltpu.VMEM((PIECE, DEPTH), bf16),
            pltpu.VMEM((2, 2, RING, RING, PIECE, DEPTH), bf16),
            pltpu.VMEM((8, ROWS, 2 * LANES), f32),
            pltpu.VMEM((ROWS, LANES), f32),
            pltpu.VMEM((ROWS, LANES), f32),
            pltpu.VMEM((16, 8, LANES), f32),
            pltpu.VMEM((8, 16, LANES), f32),
            pltpu.VMEM((8, 16, LANES), f32),
            pltpu.VMEM((8, 16, LANES), f32),
            pltpu.VMEM((8, 16, LANES), f32),
            pltpu.VMEM((4, 8, LANES), f32),
            pltpu.VMEM((4, 8, LANES), f32),
            pltpu.VMEM((16, LANES), f32),
            pltpu.VMEM((8, LANES), f32),
            dma((2,)),
            dma((32,)),
            dma((8,)),
            dma((39,)),
            dma((34,)),
            dma((34,)),
        ],
        compiler_params=pltpu.CompilerParams(
            collective_id=0, has_side_effects=True, vmem_limit_bytes=48 * 1024 * 1024
        ),
        cost_estimate=pl.CostEstimate(
            flops=2 * ROWS * 2048 * DEPTH, bytes_accessed=1 << 22, transcendentals=1 << 21
        ),
    )(sources, targets)
    return row_best.reshape(ROWS), col_best.reshape(PIECE)


def solution(mesh):
    in_specs = (P("src", None), P(("src", "tgt"), None))
    out_specs = (P("src"), P(("src", "tgt")))
    return jax.shard_map(local, mesh=mesh, in_specs=in_specs, out_specs=out_specs, check_vma=False)
```

time: 581 us -> 64.2 us (0.11)
  the two profiles are of different devices: /device:TPU:1 before, /device:TPU:32 now
where the time goes in v1:
time: 64.2 us; the launch traced here: 64 us
  Pallas kernels  59.8 us (93%)
  local copies, waits for them, and re-layouts  3.53 us (5%)
  between operations  0.65 us (1%)
    pallas_call x1, Pallas kernels, local(): pl.pallas_call(kernel, out_shape=(jax.ShapeDtypeStruct((8, LANES), f32),...  59.8 us
    unnamed x6, local copies, waits for them, and re-layouts  3.53 us

profile of v1, /device:TPU:32, one launch (start us, length us, event | category | flops | bytes accessed | tf_op | source)
XLA Modules:
  0.0 64.0 jit_solution(3734595227804636266)
XLA Ops:
  0.6 0.0 copy-start
  0.6 1.6 %copy-done = bf16[1024,1024]{1,0:T(8,128)(2,1)S(1)} copy-done((bf16[1024,1024]{1,0:T(8,128)(2,1)S(1)}, bf16[1024,1024]{1,0:T(8,128)(2,1)}, u32[]{:S(2)}) %copy-start) | copy-done | bytes 2097176
  2.2 0.0 copy-start.1
  2.2 0.8 %copy-done.1 = bf16[32,1024]{1,0:T(8,128)(2,1)S(1)} copy-done((bf16[32,1024]{1,0:T(8,128)(2,1)S(1)}, bf16[32,1024]{1,0:T(8,128)(2,1)}, u32[]{:S(2)}) %copy-start.1) | copy-done | bytes 65560
  3.1 59.8 %shard_map.41 = (f32[8,128]{1,0:T(8,128)S(1)}, f32[1,32]{1,0:T(1,128)S(1)}) custom-call(bf16[1024,1024]{1,0:T(8,128)(2,1)S(1)} %copy-done, bf16[32,1024]{1,0:T(8,128)(2,1)S(1)} %copy-done.1), custom_call_target="tpu_custom_call" | custom-call | flops 4294967296 | bytes 4194304 | tf_op jit(solution)/shard_map/pallas_call | solution.py:329
  62.9 0.6 copy.6
  63.5 0.5 copy.7
Async XLA Ops:
  0.6 1.6 %copy-start = (bf16[1024,1024]{1,0:T(8,128)(2,1)S(1)}, bf16[1024,1024]{1,0:T(8,128)(2,1)}, u32[]{:S(2)}) copy-start(bf16[1024,1024]{1,0:T(8,128)(2,1)} %src_ref.1) | copy-start | bytes 6291460
  2.2 0.8 %copy-start.1 = (bf16[32,1024]{1,0:T(8,128)(2,1)S(1)}, bf16[32,1024]{1,0:T(8,128)(2,1)}, u32[]{:S(2)}) copy-start(bf16[32,1024]{1,0:T(8,128)(2,1)} %tgt_ref.1) | copy-start | bytes 196612

commit v2 on v1

--- a/solution.py
+++ b/solution.py
@@ -15,7 +15,57 @@
 ROWS, DEPTH, PIECE = 1024, 1024, 32
 LANES = 128
 ORDER = ((0, 0), (0, -1), (0, 1), (1, 0), (0, 2), (1, -1), (1, 1), (1, 2))
-VIA_PLUS = ((0, 1), (-1, 2))
+
+
+def plan():
+    todo = []
+
+    def send(plane, step_b, step_a, *ways):
+        todo.extend(("send", plane, step_b, step_a, way) for way in ways)
+
+    def take(plane, step_b, step_a, *ways):
+        todo.append(("take", plane, step_b, step_a))
+        send(plane, step_b, step_a, *ways)
+
+    def share(*steps):
+        todo.extend(("share", step) for step in steps)
+
+    def multiply(*steps):
+        todo.extend(("multiply", step) for step in steps)
+
+    send(0, 0, 0, "z", "+a", "-a", "2a", "+b", "-b")
+    todo.append(("prepare",))
+    take(0, 0, -1, "+b", "-b")
+    take(0, 0, 1, "+b", "-b")
+    take(1, 0, 0, "+a", "-a", "2a")
+    take(0, 0, 2, "+b", "-b")
+    share(0)
+    send(1, 0, 0, "+b", "-b", "2b")
+    for d in (0, -1, 1, 2):
+        take(0, -1, d, *(("+b",) if d in (0, 1) else ()))
+        take(0, 1, d, *(() if d in (0, 1) else ("-b",)))
+    share(1, 2)
+    take(1, 0, -1, "+b", "-b")
+    take(1, 0, 1, "+b", "-b")
+    take(1, 0, 2, "+b", "-b")
+    for d in (-1, 1, 2):
+        send(1, 0, d, "2b")
+    share(3)
+    multiply(0, 1, 2)
+    for d in (0, -1, 1, 2):
+        take(0, 2, d)
+    share(4)
+    multiply(3)
+    for d in (0, -1, 1, 2):
+        take(1, -1, d)
+        take(1, 1, d)
+    share(5, 6)
+    multiply(4)
+    for d in (0, -1, 1, 2):
+        take(1, 2, d)
+    share(7)
+    multiply(5, 6, 7)
+    return todo
 
 
 def unit_rows(values):
@@ -38,8 +88,8 @@
     col_part,
     col_one,
     col_two,
-    max_one,
-    max_two,
+    col_top,
+    best_of,
     row_one,
     row_max,
     col_norm,
@@ -50,6 +100,7 @@
     send_sem,
     small_send,
     small_recv,
+    top_sem,
 ):
     s = lax.axis_index("src")
     t = lax.axis_index("tgt")
@@ -68,7 +119,7 @@
         return device(bb + c * (aa - bb), aa + c * (bb - aa), zh, c, t)
 
     other_core = device(y, x, zh, 1 - c, t)
-    other_plane = device(y, x, 1 - zh, c, 3 - t)
+    other_plane = device(y, x, 1 - zh, c, (t + 2) % 4)
 
     load = pltpu.make_async_copy(src_ref, unit, load_sem.at[0])
     load.start()
@@ -83,12 +134,14 @@
         p = (me_two + i) % 8
         q = p % 2
         other = (q - zh) * (q - zh)
-        peers_two.append(device(p // 2, x, q, c, t + other * (3 - 2 * t)))
+        peers_two.append(device(p // 2, x, q, c, (t + other * 2) % 4))
     for i in range(1, 4):
         peers_row.append(device(y, x, zh, c, (t + i) % 4))
 
     barrier = pltpu.get_barrier_semaphore()
-    for peer in peers_one + peers_two + peers_row:
+    greeted = [moved(1, 0), moved(2, 0), moved(3, 0), moved(0, 1), moved(0, 2), moved(0, 3), other_core, other_plane]
+    greeted += peers_row
+    for peer in greeted:
         pl.semaphore_signal(barrier, inc=1, device_id=peer, device_id_type=MESH)
 
     def plane_of(p):
@@ -99,7 +152,7 @@
 
     load_piece.wait()
     gathered[c, zh, b, a] = unit_rows(piece[...])
-    pl.semaphore_wait(barrier, 17)
+    pl.semaphore_wait(barrier, len(greeted))
 
     sends = []
 
@@ -138,32 +191,20 @@
 
     plus_a, minus_a, plus_b, minus_b = moved(1, 0), moved(-1, 0), moved(0, 1), moved(0, -1)
 
-    def spread(step):
-        p, db = ORDER[step]
-        for da in (0, -1, 1, 2):
-            if (p, db, da) != (0, 0, 0):
-                arrived(p, db, da)
-            if db == 0:
-                if da == 0:
-                    forward(p, 0, 0, plus_a)
-                    forward(p, 0, 0, minus_a)
-                    if p == 0:
-                        forward(p, 0, 0, other_plane)
-                if da == -1 and p == 0:
-                    forward(p, 0, da, plus_a)
-                if da == 1 and p == 1:
-                    forward(p, 0, da, minus_a)
-                forward(p, 0, da, plus_b)
-                forward(p, 0, da, minus_b)
-            elif db == -1 and da in VIA_PLUS[p]:
-                forward(p, db, da, plus_b)
-            elif db == 1 and da not in VIA_PLUS[p]:
-                forward(p, db, da, minus_b)
-            if (p, db, da) == (0, 0, 0):
-                prepare()
+    ways = {
+        "+a": plus_a,
+        "-a": minus_a,
+        "2a": moved(2, 0),
+        "+b": plus_b,
+        "-b": minus_b,
+        "2b": moved(0, 2),
+        "z": other_plane,
+    }
+
+    def share(step):
         copy = pair_copy(step, True)
         copy.start()
-        return copy
+        pair_sends.append(copy)
 
     def prepare():
         load.wait()
@@ -209,11 +250,18 @@
         col_part[mine] = total[:, :LANES]
         col_part[theirs] = total[:, LANES:]
 
-    pair_sends = [spread(0), spread(1)]
-    for step in range(8):
-        if step + 2 < 8:
-            pair_sends.append(spread(step + 2))
-        multiply(step)
+    pair_sends = []
+    for event, *at in plan():
+        if event == "take":
+            arrived(*at)
+        elif event == "send":
+            forward(*at[:3], ways[at[3]])
+        elif event == "share":
+            share(*at)
+        elif event == "multiply":
+            multiply(*at)
+        else:
+            prepare()
 
     small = []
 
@@ -282,8 +330,28 @@
         mine, theirs = lines(step)
         col_part[mine] = tops[step][:, :LANES]
         col_part[theirs] = tops[step][:, LANES:]
-    max_one[me_one] = columns(jnp.max, col_part)
-    exchange(max_one, me_one, peers_one, 17, 8)
+    col_top[...] = jnp.max(col_part[...], axis=1, keepdims=True)
+    me_all = (me_two // 2 * 4 + x) * 4 + zh * 2 + c
+    best_of[me_all] = col_top[(c * 2 + zh) * 4 + b]
+
+    def top_copy(i):
+        p = (me_all + i) % 64
+        qc, qz, qx, qy = p % 2, (p // 2) % 2, (p // 4) % 4, p // 16
+        crossed = (qz - zh) * (qz - zh)
+        return pltpu.make_async_remote_copy(
+            src_ref=col_top.at[(qc * 2 + qz) * 4 + qy + qc * (qx - qy)],
+            dst_ref=best_of.at[me_all],
+            send_sem=top_sem.at[0],
+            recv_sem=top_sem.at[1],
+            device_id=device(qy, qx, qz, qc, (t + crossed * 2) % 4),
+            device_id_type=MESH,
+        )
+
+    def send_top(i, carry):
+        top_copy(i).start()
+        return carry
+
+    lax.fori_loop(1, 64, send_top, 0)
 
     collect(col_two, me_two, 7, 7, 8)
     col_norm[...] = HALF * jnp.log(jnp.sum(col_two[...], axis=0) * (1.0 / 65536.0))
@@ -302,18 +370,21 @@
 
     lax.fori_loop(0, ROWS // 32, row_body, 0)
     row_max[t] = rows_of(row_acc, jnp.max)
-    exchange(row_max, t, peers_row, 31, 4)
-
-    collect(max_one, me_one, 7, 17, 8)
-    max_two[me_two] = jnp.max(max_one[...], axis=0)
-    exchange(max_two, me_two, peers_two, 24, 8)
-    collect(row_max, t, 3, 31, 4)
+    exchange(row_max, t, peers_row, 17, 4)
+
+    collect(row_max, t, 3, 17, 4)
     row_ref[...] = jnp.max(row_max[...], axis=0) - row_norm[...]
-    collect(max_two, me_two, 7, 24, 8)
-    best = jnp.max(max_two[...], axis=0) - col_norm[...]
-    line = (c * 2 + zh) * 4 + b
-    chosen = lax.broadcasted_iota(jnp.int32, (16, LANES), 0) == line
-    best = jnp.sum(jnp.where(chosen, best, 0.0), axis=0, keepdims=True)
+    everyone = best_of.at[pl.ds(0, 63)]
+    tops_in = pltpu.make_async_remote_copy(
+        src_ref=everyone,
+        dst_ref=everyone,
+        send_sem=top_sem.at[0],
+        recv_sem=top_sem.at[1],
+        device_id=other_core,
+        device_id_type=MESH,
+    )
+    tops_in.wait_recv()
+    best = jnp.max(best_of[...], axis=0) - col_norm[pl.ds((c * 2 + zh) * 4 + b, 1), :]
     out = jnp.zeros((1, PIECE), jnp.float32)
     for i in range(RING):
         out = jnp.where(a == i, best[:, i * PIECE : (i + 1) * PIECE], out)
@@ -321,6 +392,7 @@
 
     for copy in sends + pair_sends + small:
         copy.wait_send()
+    tops_in.wait_send()
 
 
 def local(sources, targets):
@@ -332,7 +404,7 @@
             jax.ShapeDtypeStruct((8, LANES), f32),
             jax.ShapeDtypeStruct((1, PIECE), f32),
         ),
-        in_specs=[pl.BlockSpec(memory_space=pl.ANY)] * 2,
+        in_specs=[pl.BlockSpec(memory_space=pltpu.HBM)] * 2,
         out_specs=(pl.BlockSpec(memory_space=pltpu.VMEM),) * 2,
         scratch_shapes=[
             pltpu.VMEM((ROWS, DEPTH), bf16),
@@ -344,8 +416,8 @@
             pltpu.VMEM((16, 8, LANES), f32),
             pltpu.VMEM((8, 16, LANES), f32),
             pltpu.VMEM((8, 16, LANES), f32),
-            pltpu.VMEM((8, 16, LANES), f32),
-            pltpu.VMEM((8, 16, LANES), f32),
+            pltpu.VMEM((16, 1, LANES), f32),
+            pltpu.VMEM((64, 1, LANES), f32),
             pltpu.VMEM((4, 8, LANES), f32),
             pltpu.VMEM((4, 8, LANES), f32),
             pltpu.VMEM((16, LANES), f32),
@@ -354,8 +426,9 @@
             dma((32,)),
             dma((8,)),
             dma((39,)),
-            dma((34,)),
-            dma((34,)),
+            dma((20,)),
+            dma((20,)),
+            dma((2,)),
         ],
         compiler_params=pltpu.CompilerParams(
             collective_id=0, has_side_effects=True, vmem_limit_bytes=48 * 1024 * 1024

time: 64.2 us -> 50 us (0.78)
  the two profiles are of different devices: /device:TPU:32 before, /device:TPU:1 now
where the time goes in v2:
time: 50 us; the launch traced here: 49.8 us
  Pallas kernels  45.6 us (91%)
  local copies, waits for them, and re-layouts  3.53 us (7%)
  between operations  0.65 us (1%)
    pallas_call x1, Pallas kernels, local(): pl.pallas_call(kernel, out_shape=(jax.ShapeDtypeStruct((8, LANES), f32),...  45.6 us
    unnamed x6, local copies, waits for them, and re-layouts  3.53 us

profile of v2, /device:TPU:1, one launch (start us, length us, event | category | flops | bytes accessed | tf_op | source)
XLA Modules:
  0.0 49.8 jit_solution(2813049314300051618)
XLA Ops:
  0.6 0.0 copy-start
  0.6 1.6 %copy-done = bf16[1024,1024]{1,0:T(8,128)(2,1)S(1)} copy-done((bf16[1024,1024]{1,0:T(8,128)(2,1)S(1)}, bf16[1024,1024]{1,0:T(8,128)(2,1)}, u32[]{:S(2)}) %copy-start) | copy-done | bytes 2097176
  2.2 0.0 copy-start.1
  2.2 0.8 %copy-done.1 = bf16[32,1024]{1,0:T(8,128)(2,1)S(1)} copy-done((bf16[32,1024]{1,0:T(8,128)(2,1)S(1)}, bf16[32,1024]{1,0:T(8,128)(2,1)}, u32[]{:S(2)}) %copy-start.1) | copy-done | bytes 65560
  3.1 45.6 %shard_map.41 = (f32[8,128]{1,0:T(8,128)S(1)}, f32[1,32]{1,0:T(1,128)S(1)}) custom-call(bf16[1024,1024]{1,0:T(8,128)(2,1)S(1)} %copy-done, bf16[32,1024]{1,0:T(8,128)(2,1)S(1)} %copy-done.1), custom_call_target="tpu_custom_call" | custom-call | flops 4294967296 | bytes 4194304 | tf_op jit(solution)/shard_map/pallas_call | solution.py:401
  48.7 0.6 %copy.6 = f32[1024]{0:T(1024)} copy(f32[1024]{0:T(1024)S(1)} %bitcast.2) | data formatting | bytes 8192
  49.3 0.5 %copy.7 = f32[32]{0:T(128)} copy(f32[32]{0:T(128)S(1)} %bitcast.3) | data formatting | bytes 256
Async XLA Ops:
  0.6 1.6 %copy-start = (bf16[1024,1024]{1,0:T(8,128)(2,1)S(1)}, bf16[1024,1024]{1,0:T(8,128)(2,1)}, u32[]{:S(2)}) copy-start(bf16[1024,1024]{1,0:T(8,128)(2,1)} %src_ref.1) | copy-start | bytes 6291460
  2.2 0.8 %copy-start.1 = (bf16[32,1024]{1,0:T(8,128)(2,1)S(1)}, bf16[32,1024]{1,0:T(8,128)(2,1)}, u32[]{:S(2)}) copy-start(bf16[32,1024]{1,0:T(8,128)(2,1)} %tgt_ref.1) | copy-start | bytes 196612

commit v3 on v2

--- a/solution.py
+++ b/solution.py
@@ -80,7 +80,6 @@
     row_ref,
     col_ref,
     unit,
-    piece,
     gathered,
     cosine,
     row_acc,
@@ -121,10 +120,8 @@
     other_core = device(y, x, zh, 1 - c, t)
     other_plane = device(y, x, 1 - zh, c, (t + 2) % 4)
 
-    load = pltpu.make_async_copy(src_ref, unit, load_sem.at[0])
+    load = pltpu.make_async_copy(src_ref, unit, load_sem)
     load.start()
-    load_piece = pltpu.make_async_copy(tgt_ref, piece, load_sem.at[1])
-    load_piece.start()
 
     me_one, me_two = x * 2 + c, y * 2 + zh
     peers_one, peers_two, peers_row = [], [], []
@@ -150,8 +147,7 @@
     def ring(v, d):
         return (v + d + RING) % RING
 
-    load_piece.wait()
-    gathered[c, zh, b, a] = unit_rows(piece[...])
+    gathered[c, zh, b, a] = unit_rows(tgt_ref[...])
     pl.semaphore_wait(barrier, len(greeted))
 
     sends = []
@@ -404,11 +400,10 @@
             jax.ShapeDtypeStruct((8, LANES), f32),
             jax.ShapeDtypeStruct((1, PIECE), f32),
         ),
-        in_specs=[pl.BlockSpec(memory_space=pltpu.HBM)] * 2,
+        in_specs=[pl.BlockSpec(memory_space=pl.ANY), pl.BlockSpec(memory_space=pltpu.VMEM)],
         out_specs=(pl.BlockSpec(memory_space=pltpu.VMEM),) * 2,
         scratch_shapes=[
             pltpu.VMEM((ROWS, DEPTH), bf16),
-            pltpu.VMEM((PIECE, DEPTH), bf16),
             pltpu.VMEM((2, 2, RING, RING, PIECE, DEPTH), bf16),
             pltpu.VMEM((8, ROWS, 2 * LANES), f32),
             pltpu.VMEM((ROWS, LANES), f32),
@@ -422,7 +417,7 @@
             pltpu.VMEM((4, 8, LANES), f32),
             pltpu.VMEM((16, LANES), f32),
             pltpu.VMEM((8, LANES), f32),
-            dma((2,)),
+            dma,
             dma((32,)),
             dma((8,)),
             dma((39,)),
@@ -431,7 +426,7 @@
             dma((2,)),
         ],
         compiler_params=pltpu.CompilerParams(
-            collective_id=0, has_side_effects=True, vmem_limit_bytes=48 * 1024 * 1024
+            collective_id=0, has_side_effects=True, vmem_limit_bytes=53 * 1024 * 1024
         ),
         cost_estimate=pl.CostEstimate(
             flops=2 * ROWS * 2048 * DEPTH, bytes_accessed=1 << 22, transcendentals=1 << 21

time: 50 us -> 47.9 us (0.958)
  local copies, waits for them, and re-layouts: 3.53 us -> 1.94 us
    unnamed x6 -> x4, local copies, waits for them, and re-layouts: 3.53 us -> 1.94 us
where the time goes in v3:
time: 47.9 us; the launch traced here: 47.8 us
  Pallas kernels  45.2 us (94%)
  local copies, waits for them, and re-layouts  1.94 us (4%)
  between operations  0.65 us (1%)
    pallas_call x1, Pallas kernels, local(): pl.pallas_call(kernel, out_shape=(jax.ShapeDtypeStruct((8, LANES), f32),...  45.2 us
    unnamed x4, local copies, waits for them, and re-layouts  1.94 us

profile of v3, /device:TPU:1, one launch (start us, length us, event | category | flops | bytes accessed | tf_op | source)
XLA Modules:
  0.0 47.8 jit_solution(6783700269531732048)
XLA Ops:
  0.6 0.0 copy-start
  0.6 0.8 %copy-done = bf16[32,1024]{1,0:T(8,128)(2,1)S(1)} copy-done((bf16[32,1024]{1,0:T(8,128)(2,1)S(1)}, bf16[32,1024]{1,0:T(8,128)(2,1)}, u32[]{:S(2)}) %copy-start) | copy-done | bytes 65560
  1.5 45.2 %shard_map.41 = (f32[8,128]{1,0:T(8,128)S(1)}, f32[1,32]{1,0:T(1,128)S(1)}) custom-call(bf16[1024,1024]{1,0:T(8,128)(2,1)} %src_ref.1, bf16[32,1024]{1,0:T(8,128)(2,1)S(1)} %copy-done), custom_call_target="tpu_custom_call" | custom-call | flops 4294967296 | bytes 4194304 | tf_op jit(solution)/shard_map/pallas_call | solution.py:397
  46.7 0.6 %copy.6 = f32[1024]{0:T(1024)} copy(f32[1024]{0:T(1024)S(1)} %bitcast.2) | data formatting | bytes 8192
  47.3 0.5 %copy.7 = f32[32]{0:T(128)} copy(f32[32]{0:T(128)S(1)} %bitcast.3) | data formatting | bytes 256
Async XLA Ops:
  0.6 0.8 %copy-start = (bf16[32,1024]{1,0:T(8,128)(2,1)S(1)}, bf16[32,1024]{1,0:T(8,128)(2,1)}, u32[]{:S(2)}) copy-start(bf16[32,1024]{1,0:T(8,128)(2,1)} %tgt_ref.1) | copy-start | bytes 196612

commit v4 on v2

v4 whole, which is shorter than its diff:
```python
import functools
import math

import jax
import jax.numpy as jnp
from jax import lax
from jax.experimental import pallas as pl
from jax.experimental.pallas import tpu as pltpu
from jax.sharding import PartitionSpec as P

MESH = pl.DeviceIdType.MESH
EXP_SCALE = 20.0 * math.log2(math.e)
HALF = 0.025
RING = 4
ROWS, DEPTH, PIECE = 1024, 1024, 32
LANES = 128
ORDER = ((0, 0), (0, -1), (0, 1), (1, 0), (0, 2), (1, -1), (1, 1), (1, 2))


def plan():
    todo = []
    halves = ((None,), (0, 1))

    def send(plane, step_b, step_a, *ways, half=None):
        todo.extend(("send", plane, step_b, step_a, half, way) for way in ways)

    def take(plane, step_b, step_a, *ways):
        for half in halves[plane]:
            todo.append(("take", plane, step_b, step_a, half))
            send(plane, step_b, step_a, *ways, half=half)

    def again(plane, step_b, step_a, *ways):
        for half in halves[plane]:
            send(plane, step_b, step_a, *ways, half=half)

    def share(*steps):
        todo.extend(("share", step) for step in steps)

    def multiply(*steps):
        todo.append(("multiply", *steps))

    send(0, 0, 0, "z", half=0)
    send(0, 0, 0, "z", half=1)
    send(0, 0, 0, "+a", "-a", "2a", "+b", "-b")
    todo.append(("prepare",))
    take(0, 0, -1, "+b", "-b")
    take(0, 0, 1, "+b", "-b")
    take(1, 0, 0, "+a", "-a", "2a")
    take(0, 0, 2, "+b", "-b")
    share(0)
    again(1, 0, 0, "+b", "-b", "2b")
    for d in (0, -1, 1, 2):
        take(0, -1, d, *(("+b",) if d in (0, 1) else ()))
        take(0, 1, d, *(() if d in (0, 1) else ("-b",)))
    share(1, 2)
    take(1, 0, -1, "+b", "-b")
    take(1, 0, 1, "+b", "-b")
    again(1, 0, -1, "2b")
    again(1, 0, 1, "2b")
    take(1, 0, 2, "+b", "-b", "2b")
    share(3)
    multiply(0, 1, 2)
    for d in (0, -1, 1, 2):
        take(0, 2, d)
    share(4)
    multiply(3)
    for d in (0, -1, 1, 2):
        take(1, -1, d)
        take(1, 1, d)
    share(5, 6)
    multiply(4)
    for d in (0, -1, 1, 2):
        take(1, 2, d)
    share(7)
    multiply(5, 6, 7)
    return todo


def unit_rows(values):
    values = values.astype(jnp.float32)
    scale = lax.rsqrt(jnp.mean(values * values, axis=1, keepdims=True) + 1e-06)
    return (values * scale * (1.0 / 32.0)).astype(jnp.bfloat16)


def kernel(
    src_ref,
    tgt_ref,
    row_ref,
    col_ref,
    unit,
    piece,
    gathered,
    cosine,
    row_acc,
    row_bias,
    col_part,
    col_one,
    col_two,
    col_top,
    best_of,
    row_one,
    row_max,
    col_norm,
    row_norm,
    load_sem,
    recv_sem,
    pair_sem,
    send_sem,
    small_send,
    small_recv,
    top_sem,
):
    s = lax.axis_index("src")
    t = lax.axis_index("tgt")
    c = s % 2
    zh = (s // 2) % 2
    x = (s // 4) % 4
    y = s // 16
    a = x + c * (y - x)
    b = y + c * (x - y)

    def device(y, x, zh, c, t):
        return (((y * 4 + x) * 2 + zh) * 2 + c, t)

    def moved(da, db):
        aa, bb = (a + da + RING) % RING, (b + db + RING) % RING
        return device(bb + c * (aa - bb), aa + c * (bb - aa), zh, c, t)

    def ring(v, d):
        return (v + d + RING) % RING

    other_core = device(y, x, zh, 1 - c, t)
    other_plane = device(y, x, 1 - zh, c, (t + 2) % 4)

    load_piece = pltpu.make_async_copy(tgt_ref, piece, load_sem.at[0])
    load_piece.start()
    load = pltpu.make_async_copy(src_ref, unit, load_sem.at[1])
    load.start()

    me_one, me_two = x * 2 + c, y * 2 + zh
    peers_one, from_one, peers_two, from_two, peers_row, from_row = [], [], [], [], [], []
    for dx, dc in ((2, 1), (2, 0), (1, 1), (3, 1), (1, 0), (3, 0), (0, 1)):
        core = (c + dc) % 2
        peers_one.append(device(y, ring(x, dx), zh, core, t))
        from_one.append(ring(x, -dx) * 2 + core)
    for dy, dz in ((2, 1), (1, 1), (3, 1), (0, 1), (2, 0), (1, 0), (3, 0)):
        plane = (zh + dz) % 2
        peers_two.append(device(ring(y, dy), x, plane, c, (t + 2 * dz) % 4))
        from_two.append(ring(y, -dy) * 2 + plane)
    for i in range(1, 4):
        peers_row.append(device(y, x, zh, c, (t + i) % 4))
        from_row.append((t + 4 - i) % 4)

    barrier = pltpu.get_barrier_semaphore()
    greeted = [moved(1, 0), moved(2, 0), moved(3, 0), moved(0, 1), moved(0, 2), moved(0, 3), other_core, other_plane]
    greeted += peers_row
    for peer in greeted:
        pl.semaphore_signal(barrier, inc=1, device_id=peer, device_id_type=MESH)

    def plane_of(p):
        return zh + p * (1 - 2 * zh)

    load_piece.wait()
    gathered[c, zh, b, a] = unit_rows(piece[...])
    pl.semaphore_wait(barrier, len(greeted))

    sends = []

    def chunk_copy(p, db, da, half, to, arrives_in, send):
        bb, aa = ring(b, db), ring(a, da)
        slot = gathered.at[c, plane_of(p), bb, aa]
        if half is not None:
            slot = slot.at[pl.ds(half * (PIECE // 2), PIECE // 2)]
        place = bb * RING + aa
        return pltpu.make_async_remote_copy(
            src_ref=slot,
            dst_ref=slot,
            send_sem=send_sem.at[send],
            recv_sem=recv_sem.at[place if arrives_in == 0 else 16 + 2 * place + half],
            device_id=to,
            device_id_type=MESH,
        )

    def forward(p, db, da, half, way):
        copy = chunk_copy(p, db, da, half, ways[way], 1 if way == "z" else p, len(sends))
        copy.start()
        sends.append(copy)

    def arrived(p, db, da, half):
        chunk_copy(p, db, da, half, other_core, p, 0).wait_recv()

    def pair_copy(step, mine, p, db):
        core = c if mine else 1 - c
        slot = gathered.at[core, plane_of(p), ring(b if mine else a, db)]
        return pltpu.make_async_remote_copy(
            src_ref=slot,
            dst_ref=slot,
            send_sem=send_sem.at[47 + step],
            recv_sem=pair_sem.at[step],
            device_id=other_core,
            device_id_type=MESH,
        )

    plus_a, minus_a, plus_b, minus_b = moved(1, 0), moved(-1, 0), moved(0, 1), moved(0, -1)

    ways = {
        "+a": plus_a,
        "-a": minus_a,
        "2a": moved(2, 0),
        "+b": plus_b,
        "-b": minus_b,
        "2b": moved(0, 2),
        "z": other_plane,
    }

    def share(step):
        copy = pair_copy(step, True, *ORDER[step])
        copy.start()
        pair_sends.append(copy)

    def prepare():
        load.wait()

        def body(i, carry):
            rows = pl.ds(pl.multiple_of(i * 64, 64), 64)
            unit[rows, :] = unit_rows(unit[rows, :])
            return carry

        lax.fori_loop(0, ROWS // 64, body, 0)
        row_acc[...] = jnp.zeros_like(row_acc)

    def lines(p, db):
        pp = plane_of(p)
        return (pp * 2 + c) * 4 + ring(b, db), (pp * 2 + 1 - c) * 4 + ring(a, db)

    def multiply_one(step, p, db):
        pair_copy(step, False, p, db).wait_recv()
        pp = plane_of(p)
        group = jnp.concatenate(
            [
                gathered[c, pp, ring(b, db)].reshape(LANES, DEPTH),
                gathered[1 - c, pp, ring(a, db)].reshape(LANES, DEPTH),
            ],
            axis=0,
        )
        mine, theirs = lines(p, db)
        angle = lax.dot_general(
            unit[...], group, (((1,), (1,)), ((), ())), preferred_element_type=jnp.float32
        )
        cosine[step] = angle
        share = jnp.exp2(angle * EXP_SCALE)
        row_acc[...] += share[:, :LANES] + share[:, LANES:]
        total = jnp.sum(share.reshape(ROWS // 8, 8, 2 * LANES), axis=0)
        col_part[mine] = total[:, :LANES]
        col_part[theirs] = total[:, LANES:]

    def multiply(*steps):
        if len(steps) == 1:
            multiply_one(steps[0], *ORDER[steps[0]])
            return

        def body(i, carry):
            p, db = ORDER[steps[0]]
            for k in range(1, len(steps)):
                p = jnp.where(i == k, ORDER[steps[k]][0], p)
                db = jnp.where(i == k, ORDER[steps[k]][1], db)
            multiply_one(steps[0] + i, p, db)
            return carry

        lax.fori_loop(0, len(steps), body, 0)

    small = []

    def exchange(slot, peers, base):
        for i, peer in enumerate(peers):
            copy = pltpu.make_async_remote_copy(
                src_ref=slot,
                dst_ref=slot,
                send_sem=small_send.at[base + i],
                recv_sem=small_recv.at[base + i],
                device_id=peer,
                device_id_type=MESH,
            )
            copy.start()
            small.append(copy)

    def collect(slots, base):
        for i, slot in enumerate(slots):
            pltpu.make_async_remote_copy(
                src_ref=slot,
                dst_ref=slot,
                send_sem=small_send.at[base + i],
                recv_sem=small_recv.at[base + i],
                device_id=other_core,
                device_id_type=MESH,
            ).wait_recv()

    def first_stage():
        col_one[me_one] = jnp.sum(col_part[...], axis=1)
        exchange(col_one.at[me_one], peers_one, 0)

    def second_stage():
        collect([col_one.at[i] for i in from_one], 0)
        col_two[me_two] = jnp.sum(col_one[...], axis=0)
        exchange(col_two.at[me_two], peers_two, 7)

    pair_sends = []
    for event, *at in plan():
        if event == "take":
            arrived(*at)
        elif event == "send":
            forward(*at)
        elif event == "share":
            share(*at)
        elif event == "multiply":
            multiply(*at)
        else:
            prepare()

    def rows_of(source, reduce):
        parts = []
        for i in range(8):
            block = source[i * LANES : (i + 1) * LANES, :]
            parts.append(reduce(block.T, axis=0, keepdims=True))
        return jnp.concatenate(parts, axis=0)

    first_stage()
    row_one[t] = rows_of(row_acc, jnp.sum)
    exchange(row_one.at[t], peers_row, 14)
    for copy in sends + pair_sends:
        copy.wait_send()
    second_stage()

    collect([row_one.at[i] for i in from_row], 14)
    row_norm[...] = HALF * jnp.log(jnp.sum(row_one[...], axis=0) * (1.0 / 8192.0))
    for i in range(8):
        line = jnp.broadcast_to(row_norm[i : i + 1, :], (LANES, LANES))
        row_bias[i * LANES : (i + 1) * LANES, :] = line.T

    def col_body(i, tops):
        rows = pl.ds(pl.multiple_of(i * 32, 32), 32)
        bias = row_bias[rows, :]
        bias = jnp.concatenate([bias, bias], axis=1)
        new = []
        for step in range(8):
            value = (cosine[step, rows, :] - bias).reshape(4, 8, 2 * LANES)
            new.append(jnp.maximum(tops[step], jnp.max(value, axis=0)))
        return tuple(new)

    start = jnp.full((8, 2 * LANES), -1e30, jnp.float32)
    tops = lax.fori_loop(0, ROWS // 32, col_body, (start,) * 8)
    for step in range(8):
        mine, theirs = lines(*ORDER[step])
        col_part[mine] = tops[step][:, :LANES]
        col_part[theirs] = tops[step][:, LANES:]
    col_top[...] = jnp.max(col_part[...], axis=1, keepdims=True)
    me_all = (me_two // 2 * 4 + x) * 4 + zh * 2 + c
    best_of[me_all] = col_top[(zh * 2 + c) * 4 + b]

    def send_top(qy, qx, qz, qc, qt):
        pltpu.make_async_remote_copy(
            src_ref=col_top.at[(qz * 2 + qc) * 4 + qy + qc * (qx - qy)],
            dst_ref=best_of.at[me_all],
            send_sem=top_sem.at[0],
            recv_sem=top_sem.at[1],
            device_id=device(qy, qx, qz, qc, qt),
            device_id_type=MESH,
        ).start()

    spots = []
    for dx in (2, 1, 3, 0):
        for dz in (1, 0):
            for dc in (1, 0):
                spots.append((ring(x, dx), (zh + dz) % 2, (c + dc) % 2, (t + 2 * dz) % 4))

    def send_tops(dy, carry):
        for spot in spots[:-1]:
            send_top(ring(y, dy), *spot)
        return carry

    lax.fori_loop(0, RING, send_tops, 0)
    for dy in (1, 2, 3):
        send_top(ring(y, dy), *spots[-1])

    collect([col_two.at[i] for i in from_two], 7)
    col_norm[...] = HALF * jnp.log(jnp.sum(col_two[...], axis=0) * (1.0 / 65536.0))

    def row_body(i, carry):
        rows = pl.ds(pl.multiple_of(i * 32, 32), 32)
        top = None
        for step in range(8):
            mine, theirs = lines(*ORDER[step])
            value = cosine[step, rows, :]
            for part, line in ((value[:, :LANES], mine), (value[:, LANES:], theirs)):
                part = part - col_norm[pl.ds(line, 1), :]
                top = part if top is None else jnp.maximum(top, part)
        row_acc[rows, :] = top
        return carry

    lax.fori_loop(0, ROWS // 32, row_body, 0)
    row_max[t] = rows_of(row_acc, jnp.max)
    exchange(row_max.at[t], peers_row, 17)

    for copy in small:
        copy.wait_send()
    collect([row_max.at[i] for i in from_row], 17)
    row_ref[...] = jnp.max(row_max[...], axis=0) - row_norm[...]
    everyone = best_of.at[pl.ds(0, 63)]
    tops_in = pltpu.make_async_remote_copy(
        src_ref=everyone,
        dst_ref=everyone,
        send_sem=top_sem.at[0],
        recv_sem=top_sem.at[1],
        device_id=other_core,
        device_id_type=MESH,
    )
    tops_in.wait_recv()
    best = jnp.max(best_of[...], axis=0) - col_norm[pl.ds((zh * 2 + c) * 4 + b, 1), :]
    out = jnp.zeros((1, PIECE), jnp.float32)
    for i in range(RING):
        out = jnp.where(a == i, best[:, i * PIECE : (i + 1) * PIECE], out)
    col_ref[...] = out

    tops_in.wait_send()


def local(sources, targets):
    f32, bf16 = jnp.float32, jnp.bfloat16
    dma = pltpu.SemaphoreType.DMA
    row_best, col_best = pl.pallas_call(
        kernel,
        out_shape=(
            jax.ShapeDtypeStruct((8, LANES), f32),
            jax.ShapeDtypeStruct((1, PIECE), f32),
        ),
        in_specs=[pl.BlockSpec(memory_space=pl.ANY)] * 2,
        out_specs=(pl.BlockSpec(memory_space=pltpu.VMEM),) * 2,
        scratch_shapes=[
            pltpu.VMEM((ROWS, DEPTH), bf16),
            pltpu.VMEM((PIECE, DEPTH), bf16),
            pltpu.VMEM((2, 2, RING, RING, PIECE, DEPTH), bf16),
            pltpu.VMEM((8, ROWS, 2 * LANES), f32),
            pltpu.VMEM((ROWS, LANES), f32),
            pltpu.VMEM((ROWS, LANES), f32),
            pltpu.VMEM((16, 8, LANES), f32),
            pltpu.VMEM((8, 16, LANES), f32),
            pltpu.VMEM((8, 16, LANES), f32),
            pltpu.VMEM((16, 1, LANES), f32),
            pltpu.VMEM((64, 1, LANES), f32),
            pltpu.VMEM((4, 8, LANES), f32),
            pltpu.VMEM((4, 8, LANES), f32),
            pltpu.VMEM((16, LANES), f32),
            pltpu.VMEM((8, LANES), f32),
            dma((2,)),
            dma((48,)),
            dma((8,)),
            dma((55,)),
            dma((20,)),
            dma((20,)),
            dma((2,)),
        ],
        compiler_params=pltpu.CompilerParams(
            collective_id=0, has_side_effects=True, vmem_limit_bytes=55193 * 1024
        ),
        cost_estimate=pl.CostEstimate(
            flops=2 * ROWS * 2048 * DEPTH, bytes_accessed=1 << 22, transcendentals=1 << 21
        ),
    )(sources, targets)
    return row_best.reshape(ROWS), col_best.reshape(PIECE)


def solution(mesh):
    in_specs = (P("src", None), P(("src", "tgt"), None))
    out_specs = (P("src"), P(("src", "tgt")))
    return jax.shard_map(local, mesh=mesh, in_specs=in_specs, out_specs=out_specs, check_vma=False)
```

time: 50 us -> 46.1 us (0.922)
  local copies, waits for them, and re-layouts: 3.53 us -> 1.11 us
  Pallas kernels: 45.6 us -> 44.3 us
    unnamed x6 -> x2, local copies, waits for them, and re-layouts: 3.53 us -> 1.11 us
    pallas_call x1, Pallas kernels: 45.6 us -> 44.3 us  [local(): pl.pallas_call(kernel, out_shape=(jax.ShapeDtypeStruct((8, LANES), f32),...]
where the time goes in v4:
time: 46.1 us; the launch traced here: 46 us
  Pallas kernels  44.3 us (96%)
  local copies, waits for them, and re-layouts  1.11 us (2%)
  between operations  0.64 us (1%)
    pallas_call x1, Pallas kernels, local(): pl.pallas_call(kernel, out_shape=(jax.ShapeDtypeStruct((8, LANES), f32),...  44.3 us
    unnamed x2, local copies, waits for them, and re-layouts  1.11 us

profile of v4, /device:TPU:1, one launch (start us, length us, event | category | flops | bytes accessed | tf_op | source)
XLA Modules:
  0.0 46.0 jit_solution(4198341552894394166)
XLA Ops:
  0.6 44.3 %shard_map.41 = (f32[8,128]{1,0:T(8,128)S(1)}, f32[1,32]{1,0:T(1,128)S(1)}) custom-call(bf16[1024,1024]{1,0:T(8,128)(2,1)} %src_ref.1, bf16[32,1024]{1,0:T(8,128)(2,1)} %tgt_ref.1), custom_call_target="tpu_custom_call" | custom-call | flops 4294967296 | bytes 4194304 | tf_op jit(solution)/shard_map/pallas_call | solution.py:430
  44.9 0.6 %copy.6 = f32[1024]{0:T(1024)} copy(f32[1024]{0:T(1024)S(1)} %bitcast.2) | data formatting | bytes 8192
  45.5 0.5 %copy.7 = f32[32]{0:T(128)} copy(f32[32]{0:T(128)S(1)} %bitcast.3) | data formatting | bytes 256

commit v5 on v4

--- a/solution.py
+++ b/solution.py
@@ -55,18 +55,20 @@
     share(1, 2)
     take(1, 0, -1, "+b", "-b")
     take(1, 0, 1, "+b", "-b")
-    again(1, 0, -1, "2b")
-    again(1, 0, 1, "2b")
     take(1, 0, 2, "+b", "-b", "2b")
     share(3)
     multiply(0, 1, 2)
+    take(1, -1, -1, "+b")
+    take(1, 1, 1, "-b")
     for d in (0, -1, 1, 2):
         take(0, 2, d)
     share(4)
     multiply(3)
     for d in (0, -1, 1, 2):
-        take(1, -1, d)
-        take(1, 1, d)
+        if d != -1:
+            take(1, -1, d)
+        if d != 1:
+            take(1, 1, d)
     share(5, 6)
     multiply(4)
     for d in (0, -1, 1, 2):

time: 46.1 us -> 45.1 us (0.978)
  Pallas kernels: 44.3 us -> 43.1 us
    pallas_call x1, Pallas kernels: 44.3 us -> 43.1 us  [local(): pl.pallas_call(kernel, out_shape=(jax.ShapeDtypeStruct((8, LANES), f32),...]
where the time goes in v5:
time: 45.1 us; the launch traced here: 44.9 us
  Pallas kernels  43.1 us (96%)
  local copies, waits for them, and re-layouts  1.11 us (2%)
  between operations  0.64 us (1%)
    pallas_call x1, Pallas kernels, local(): pl.pallas_call(kernel, out_shape=(jax.ShapeDtypeStruct((8, LANES), f32),...  43.1 us
    unnamed x2, local copies, waits for them, and re-layouts  1.11 us

profile of v5, /device:TPU:1, one launch (start us, length us, event | category | flops | bytes accessed | tf_op | source)
XLA Modules:
  0.0 44.9 jit_solution(9121695850886228582)
XLA Ops:
  0.6 43.1 %shard_map.41 = (f32[8,128]{1,0:T(8,128)S(1)}, f32[1,32]{1,0:T(1,128)S(1)}) custom-call(bf16[1024,1024]{1,0:T(8,128)(2,1)} %src_ref.1, bf16[32,1024]{1,0:T(8,128)(2,1)} %tgt_ref.1), custom_call_target="tpu_custom_call" | custom-call | flops 4294967296 | bytes 4194304 | tf_op jit(solution)/shard_map/pallas_call | solution.py:432
  43.8 0.6 %copy.6 = f32[1024]{0:T(1024)} copy(f32[1024]{0:T(1024)S(1)} %bitcast.2) | data formatting | bytes 8192
  44.4 0.5 %copy.7 = f32[32]{0:T(128)} copy(f32[32]{0:T(128)S(1)} %bitcast.3) | data formatting | bytes 256

commit v6 on v5

--- a/solution.py
+++ b/solution.py
@@ -81,7 +81,7 @@
 def unit_rows(values):
     values = values.astype(jnp.float32)
     scale = lax.rsqrt(jnp.mean(values * values, axis=1, keepdims=True) + 1e-06)
-    return (values * scale * (1.0 / 32.0)).astype(jnp.bfloat16)
+    return (values * (scale * (1.0 / 32.0))).astype(jnp.bfloat16)
 
 
 def kernel(
@@ -387,16 +387,20 @@
     collect([col_two.at[i] for i in from_two], 7)
     col_norm[...] = HALF * jnp.log(jnp.sum(col_two[...], axis=0) * (1.0 / 65536.0))
 
+    norms = []
+    for step in range(8):
+        for line in lines(*ORDER[step]):
+            norms.append(jnp.broadcast_to(col_norm[pl.ds(line, 1), :], (8, LANES)))
+
     def row_body(i, carry):
         rows = pl.ds(pl.multiple_of(i * 32, 32), 32)
         top = None
         for step in range(8):
-            mine, theirs = lines(*ORDER[step])
             value = cosine[step, rows, :]
-            for part, line in ((value[:, :LANES], mine), (value[:, LANES:], theirs)):
-                part = part - col_norm[pl.ds(line, 1), :]
+            for k in range(2):
+                part = value[:, k * LANES : (k + 1) * LANES].reshape(4, 8, LANES) - norms[2 * step + k]
                 top = part if top is None else jnp.maximum(top, part)
-        row_acc[rows, :] = top
+        row_acc[rows, :] = top.reshape(32, LANES)
         return carry
 
     lax.fori_loop(0, ROWS // 32, row_body, 0)

time: 45.1 us -> 44.9 us (level)
  no operation moved by 1% of the time
where the time goes in v6:
time: 44.9 us; the launch traced here: 44.7 us
  Pallas kernels  43 us (96%)
  local copies, waits for them, and re-layouts  1.11 us (2%)
  between operations  0.64 us (1%)
    pallas_call x1, Pallas kernels, local(): pl.pallas_call(kernel, out_shape=(jax.ShapeDtypeStruct((8, LANES), f32),...  43 us
    unnamed x2, local copies, waits for them, and re-layouts  1.11 us

profile of v6, /device:TPU:1, one launch (start us, length us, event | category | flops | bytes accessed | tf_op | source)
XLA Modules:
  0.0 44.7 jit_solution(4667483088527953673)
XLA Ops:
  0.6 43.0 %shard_map.41 = (f32[8,128]{1,0:T(8,128)S(1)}, f32[1,32]{1,0:T(1,128)S(1)}) custom-call(bf16[1024,1024]{1,0:T(8,128)(2,1)} %src_ref.1, bf16[32,1024]{1,0:T(8,128)(2,1)} %tgt_ref.1), custom_call_target="tpu_custom_call" | custom-call | flops 4294967296 | bytes 4194304 | tf_op jit(solution)/shard_map/pallas_call | solution.py:436
  43.6 0.6 %copy.6 = f32[1024]{0:T(1024)} copy(f32[1024]{0:T(1024)S(1)} %bitcast.2) | data formatting | bytes 8192
  44.2 0.5 %copy.7 = f32[32]{0:T(128)} copy(f32[32]{0:T(128)S(1)} %bitcast.3) | data formatting | bytes 256
